TPU v7x, 512 devices: a whole 4x4x16 slice. The times are simulated.
512 devices in a mesh: dp: 16 (over y, x), expert: 32 (over z, core).
Axes of the slice: x: 4, y: 4, z: 16, core: 2. Of those that a mesh axis runs over, the one named last changes fastest.
Arguments:
- tokens: bfloat16 [65536, 512], P(('dp', 'expert')), may hold values from -6 to 6
- cotangent: bfloat16 [65536, 512], P(('dp', 'expert')), may hold values from -0.29882812 to 0.29882812
- labels: int32 [65536, 1], P(('dp', 'expert')), may hold values from 0 to 63; in each aligned block of 128 rows (0 to 127, 128 to 255, ...) at most 4 rows name the same one
- placement: int32 [64], replicated, may hold values from 0 to 63, each once
- mass: float32 [65536], P(('dp', 'expert')), may hold values from 0.1 to 10
- w_head: float32 [512, 16], replicated, may hold values from -0.25 to 0.25
- w_up: bfloat16 [64, 512, 2048], P('expert', None, 'dp'), may hold values from -0.25 to 0.25
- w_down: bfloat16 [64, 2048, 512], P('expert', 'dp'), may hold values from -0.125 to 0.125
- up_moment: bfloat16 [64, 512, 2048], P('expert', None, 'dp'), may hold values from -2 to 2
- up_square: bfloat16 [64, 512, 2048], P('expert', None, 'dp'), may hold values from 0.0099487305 to 1
- down_moment: bfloat16 [64, 2048, 512], P('expert', 'dp'), may hold values from -2 to 2
- down_square: bfloat16 [64, 2048, 512], P('expert', 'dp'), may hold values from 0.0099487305 to 1
Outputs:
- fine_precip: float32 [65536, 16], P(('dp', 'expert'))
- up_next: bfloat16 [64, 512, 2048], P('expert', None, 'dp')
- down_next: bfloat16 [64, 2048, 512], P('expert', 'dp')
- up_moment_next: bfloat16 [64, 512, 2048], P('expert', None, 'dp')
- up_square_next: bfloat16 [64, 512, 2048], P('expert', None, 'dp')
- down_moment_next: bfloat16 [64, 2048, 512], P('expert', 'dp')
- down_square_next: bfloat16 [64, 2048, 512], P('expert', 'dp')
Inputs may be any that keep to these rules, and one draw needn't show every extreme that they name: `labels`: within each device's block of 128 rows no regime is named more than 4 times, and in every draw some regime is named exactly 4 times in some block; every regime is named somewhere. `placement`: each regime stands in exactly one expert slot.
All inputs are finite; a program needn't handle non-finite values.
Results may differ from a plain program's by a relative error of at most 0.0045.
Values may be sent and summed in bfloat16 or wider, within the bound.
A program may use at most 64 MiB of HBM per device.

v0:
```python
import jax
import jax.numpy as jnp
from jax import lax
from jax.sharding import PartitionSpec as P

CAP = 4
beta_first = 0.9
beta_second = 0.95
correct_first = 1.0 - 0.9**20
correct_second = 1.0 - 0.95**20
learn_rate = 0.002
adam_epsilon = 1e-08


def gelu_parts(pre):
    normal_cdf = 0.5 * (1.0 + lax.erf(pre * 0.7071067811865476))
    density = jnp.exp(-0.5 * pre * pre) * 0.3989422804014327
    return (pre * normal_cdf, normal_cdf + pre * density)


def adam_step(weight, first, second, grad):
    new_first = beta_first * first.astype(jnp.float32) + (1.0 - beta_first) * grad
    new_second = beta_second * second.astype(jnp.float32) + (1.0 - beta_second) * grad * grad
    update = new_first / correct_first / (jnp.sqrt(new_second / correct_second) + adam_epsilon)
    moved = weight.astype(jnp.float32) - learn_rate * update
    return (
        moved.astype(jnp.bfloat16),
        new_first.astype(jnp.bfloat16),
        new_second.astype(jnp.bfloat16),
    )


def route_slots(labels, placement, capacity, holders, local_count):
    experts = placement.shape[0]
    regimes = jnp.arange(experts, dtype=jnp.int32)
    owner = jnp.sum(jnp.where(placement[None, :] == regimes[:, None], regimes[None, :], 0), axis=1)
    chosen = labels[:, 0][:, None] == regimes[None, :]
    target = jnp.sum(jnp.where(chosen, owner[None, :], 0), axis=1)
    onehot = (target[:, None] == regimes[None, :]).astype(jnp.int32)
    earlier = jnp.cumsum(onehot, axis=0) - onehot
    position = jnp.sum(earlier * onehot, axis=1)
    lane_index = target % local_count * holders + target // local_count
    return lane_index * capacity + position


def fill_slots(values, slots, count):
    row_count = values.shape[0]
    source = (
        jnp.full((count,), row_count, jnp.int32)
        .at[slots]
        .set(jnp.arange(row_count, dtype=jnp.int32))
    )
    padded = jnp.concatenate([values, jnp.zeros((1, values.shape[1]), values.dtype)], axis=0)
    return jnp.take(padded, source, axis=0)


def expert_rows(rows_x, rows_grad, w_in, w_out):
    pre = jnp.einsum("krd,kdf->krf", rows_x, w_in, preferred_element_type=jnp.float32)
    value, slope = gelu_parts(pre)
    hidden = value.astype(jnp.bfloat16)
    back = jnp.einsum("krd,kfd->krf", rows_grad, w_out, preferred_element_type=jnp.float32)
    hidden_grad = (back * slope).astype(jnp.bfloat16)
    return (hidden, hidden_grad)


def outer_in(rows_x, hidden_grad):
    return jnp.einsum("krd,krf->kdf", rows_x, hidden_grad, preferred_element_type=jnp.float32)


def outer_out(hidden, rows_grad):
    return jnp.einsum("krf,krd->kfd", hidden, rows_grad, preferred_element_type=jnp.float32)


def local(
    tokens,
    cotangent,
    labels,
    placement,
    mass,
    w_head,
    w_up,
    w_down,
    up_moment,
    up_square,
    down_moment,
    down_square,
):
    capacity = CAP
    experts = placement.shape[0]
    width = tokens.shape[1]
    local_count = w_up.shape[0]
    holders = lax.axis_size("expert")
    slots = route_slots(labels, placement, capacity, holders, local_count)
    slot_count = experts * capacity
    recv_rows = holders * capacity
    send_x = fill_slots(tokens, slots, slot_count).reshape(local_count, holders, capacity, width)
    send_grad = fill_slots(cotangent, slots, slot_count).reshape(
        local_count, holders, capacity, width
    )
    recv_x, recv_grad = (
        lax.all_to_all(send_x, "expert", split_axis=1, concat_axis=1, tiled=True),
        lax.all_to_all(send_grad, "expert", split_axis=1, concat_axis=1, tiled=True),
    )
    recv_x = recv_x.reshape(local_count, recv_rows, width)
    recv_grad = recv_grad.reshape(local_count, recv_rows, width)
    piece_x = lax.all_gather(recv_x, "dp", axis=1, tiled=True)
    piece_grad = lax.all_gather(recv_grad, "dp", axis=1, tiled=True)
    hidden, hidden_grad = expert_rows(piece_x, piece_grad, w_up, w_down)
    grad_in = outer_in(piece_x, hidden_grad)
    grad_out = outer_out(hidden, piece_grad)
    absorb_hidden_all = jnp.swapaxes(hidden, 0, 1)
    hidden_all, grad_in, grad_out = (absorb_hidden_all, grad_in, grad_out)
    summed = lax.psum_scatter(
        jnp.einsum("rkf,kfd->rkd", hidden_all, w_down, preferred_element_type=jnp.float32).astype(
            jnp.bfloat16
        ),
        "dp",
        scatter_dimension=0,
        tiled=True,
    )
    outgoing = jnp.swapaxes(summed, 0, 1).reshape(local_count, holders, capacity, width)
    returned = lax.all_to_all(outgoing, "expert", split_axis=1, concat_axis=1, tiled=True)
    expert_out = jnp.take(returned.reshape(slot_count, width), slots, axis=0)
    field = tokens.astype(jnp.float32) + expert_out.astype(jnp.float32)
    logits = jnp.dot(
        field, w_head, precision=lax.Precision.HIGHEST, preferred_element_type=jnp.float32
    )
    positive = jax.nn.softplus(logits) + 0.1
    fine_precip = mass[:, None] * positive / jnp.sum(positive, axis=1, keepdims=True)
    up_next, up_moment_next, up_square_next = adam_step(w_up, up_moment, up_square, grad_in)
    down_next, down_moment_next, down_square_next = adam_step(
        w_down, down_moment, down_square, grad_out
    )
    return (
        fine_precip,
        up_next,
        down_next,
        up_moment_next,
        up_square_next,
        down_moment_next,
        down_square_next,
    )


def solution(mesh):
    placed = (
        P(("dp", "expert"), None),
        P(("dp", "expert"), None),
        P(("dp", "expert"), None),
        P(),
        P(("dp", "expert")),
        P(),
        P("expert", None, "dp"),
        P("expert", "dp", None),
        P("expert", None, "dp"),
        P("expert", None, "dp"),
        P("expert", "dp", None),
        P("expert", "dp", None),
    )
    return jax.shard_map(
        local,
        mesh=mesh,
        in_specs=placed,
        out_specs=(
            P(("dp", "expert"), None),
            P("expert", None, "dp"),
            P("expert", "dp", None),
            P("expert", None, "dp"),
            P("expert", None, "dp"),
            P("expert", "dp", None),
            P("expert", "dp", None),
        ),
        check_vma=False,
    )
```

profile of v0, /device:TPU:1, one launch (start us, length us, event | category | flops | bytes accessed | tf_op | source)
XLA Modules:
  0.0 303.4 jit_solution(4484119608090613356)
XLA Ops:
  7.2 0.0 copy-start
  7.2 0.0 all-gather.3.cloned.1.call-start
  7.2 0.8 select_reduce_fusion.2
  8.0 0.8 select_reduce_fusion.1
  8.8 0.1 fusion.28
  8.9 0.2 reduce_window_sum.11
  9.1 0.2 select_reduce_fusion
  9.3 1.0 scatter_custom_fusion
  10.3 0.9 concatenate.7
  11.3 0.9 concatenate.6
  12.2 1.2 gather_fusion.2
  13.3 1.2 gather_fusion.1
  14.5 0.0 copy-start.2
  14.5 0.1 broadcast_select_fusion
  14.6 0.1 reshape.141
  14.7 0.1 copy.29
  14.8 38.5 %all_to_all.15 = bf16[2,32,4,512]{3,2,0,1:T(4,128)(2,1)S(1)} all-to-all(bf16[2,32,4,512]{3,2,0,1:T(4,128)(2,1)S(1)} %copy.29), channel_id=1, replica_groups=mesh['dp'=16,'expert'=32] {'expert'}, dimensions={1} | all-to-all | bytes 524288 | tf_op jit(solution)/shard_map/all_to_all | solution.py:101
  53.3 0.1 copy.30
  53.4 0.8 reshape.142
  54.2 0.0 all-gather.3.cloned.1.call-update
  54.2 0.0 copy-start.1
  54.2 0.0 reduce-scatter.2.cloned.1.call-start
  54.3 58.6 %all-gather.3.cloned.1.call-done = bf16[2,2048,512]{2,1,0:T(8,128)(2,1)} async-done(((bf16[2,128,512]{2,1,0:T(8,128)(2,1)}), bf16[2,2048,512]{2,1,0:T(8,128)(2,1)}) %all-gather.3.cloned.1.call-update) | async-done | bytes 4194320 | tf_op jit(solution)/shard_map/all_gather | solution.py:106
  112.9 0.0 copy-done.2
  112.9 3.4 %fusion.46 = f32[2,2048,128]{2,1,0:T(8,128)S(1)} fusion(bf16[2,2048,512]{2,1,0:T(8,128)(2,1)} %all-gather.3.cloned.1.call-done, bf16[2,512,128]{2,1,0:T(8,128)(2,1)S(1)} %copy-done.2), kind=kOutput, calls=%fused_computation.89 | convolution fusion | flops 536870912 | bytes 6553600 | tf_op jit(solution)/shard_map/krd,kdf->krf/dot_general | solution.py:58
  116.4 0.0 copy-done.1
  116.4 3.2 %convert_bitcast_fusion = bf16[2048,2,512]{2,0,1:T(8,128)(2,1)} fusion(bf16[2,128,512]{2,1,0:T(8,128)(2,1)S(1)} %copy-done.1, f32[2,2048,128]{2,1,0:T(8,128)S(1)} %fusion.46), kind=kOutput, calls=%fused_computation.4 | convolution fusion | flops 541589504 | bytes 6553600 | tf_op jit(solution)/shard_map/rkf,kfd->rkd/dot_general | solution.py:114
  119.6 0.0 reduce-scatter.2.cloned.1.call-update
  119.6 0.0 all-gather.5.cloned.1.call-start
  119.6 0.1 reshape.145
  119.7 0.0 copy-start.5
  119.7 0.0 copy-start.6
  119.7 0.1 copy.33
  119.8 34.9 %all_to_all.16 = bf16[2,32,4,512]{3,2,0,1:T(4,128)(2,1)S(1)} all-to-all(bf16[2,32,4,512]{3,2,0,1:T(4,128)(2,1)S(1)} %copy.33), channel_id=1, replica_groups=mesh['dp'=16,'expert'=32] {'expert'}, dimensions={1} | all-to-all | bytes 524288 | tf_op jit(solution)/shard_map/all_to_all | solution.py:102
  154.8 0.1 copy.34
  154.9 0.8 reshape.146
  155.6 0.0 all-gather.5.cloned.1.call-update
  155.7 55.1 %reduce-scatter.2.cloned.1.call-done = bf16[128,2,512]{2,0,1:T(8,128)(2,1)} async-done(((bf16[2048,2,512]{2,0,1:T(8,128)(2,1)}), bf16[128,2,512]{2,0,1:T(8,128)(2,1)}) %reduce-scatter.2.cloned.1.call-update) | async-done | bytes 262160 | tf_op jit(solution)/shard_map/reduce_scatter | solution.py:113
  210.8 1.0 reshape.143
  211.8 0.8 copy.31
  212.6 14.6 %all-to-all-start.1 = ((bf16[2,32,4,512]{3,2,0,1:T(4,128)(2,1)}), bf16[2,32,4,512]{3,2,0,1:T(4,128)(2,1)S(1)}, u32[]{:S(2)}, u32[]{:S(2)}) async-start(bf16[2,32,4,512]{3,2,0,1:T(4,128)(2,1)} %copy.31), calls=%async_computation.2 | async-start | bytes 524288 | tf_op jit(solution)/shard_map/all_to_all | solution.py:122
  227.3 55.6 %all-gather.5.cloned.1.call-done = bf16[2,2048,512]{2,1,0:T(8,128)(2,1)} async-done(((bf16[2,128,512]{2,1,0:T(8,128)(2,1)}), bf16[2,2048,512]{2,1,0:T(8,128)(2,1)}) %all-gather.5.cloned.1.call-update) | async-done | bytes 4194320 | tf_op jit(solution)/shard_map/all_gather | solution.py:107
  282.9 0.0 copy-done.5
  282.9 0.0 copy-done.6
  282.9 4.4 %fusion.19 = (bf16[2,128,512]{2,1,0:T(8,128)(2,1)}, bf16[2,128,512]{2,1,0:T(8,128)(2,1)}, bf16[2,128,512]{2,1,0:T(8,128)(2,1)}) fusion(bf16[2,128,512]{2,1,0:T(8,128)(2,1)S(1)} %copy-done.5, bf16[2,128,512]{2,1,0:T(8,128)(2,1)S(1)} %copy-done.6, bf16[2,128,512]{2,1,0:T(8,128)(2,1)S(1)} %copy-done.1, bf16[2,2048,512]{2,1,0:T(8,128)(2,1)} %all-gather.5.cloned.1.call-done, ...), kind=kOutput, calls=%fused_computation.35 | convolution fusion | flops 541982720 | bytes 7864320 | tf_op jit(solution)/shard_map/krf,krd->kfd/dot_general | solution.py:71
  287.3 7.5 %fusion.20 = (bf16[2,512,128]{2,1,0:T(8,128)(2,1)}, bf16[2,512,128]{2,1,0:T(8,128)(2,1)}, bf16[2,512,128]{2,1,0:T(8,128)(2,1)}) fusion(bf16[2,512,128]{2,1,0:T(8,128)(2,1)} %param.23, bf16[2,512,128]{2,1,0:T(8,128)(2,1)} %param.22, bf16[2,512,128]{2,1,0:T(8,128)(2,1)S(1)} %copy-done.2, bf16[2,2048,512]{2,1,0:T(8,128)(2,1)} %all-gather.3.cloned.1.call-done, ...), kind=kOutput, calls=%fused_computation.36 | convolution fusion | flops 1081475072 | bytes 12320768 | tf_op jit(solution)/shard_map/krd,krf->kdf/dot_general | solution.py:67
  294.7 0.0 copy-start.3
  294.7 0.0 copy-start.4
  294.7 0.0 all-to-all-done.1
  294.7 0.1 copy.32
  294.8 0.1 reshape.144
  294.9 0.8 gather_fusion
  295.7 0.0 copy-done
  295.8 0.0 copy-done.3
  295.8 0.5 fusion.45
  296.2 0.0 copy-done.4
  296.2 0.6 multiply_divide_fusion
  (7 shorter events, 0.1 us)
Async XLA Ops:
  7.2 288.6 %copy-start = (f32[512,16]{0,1:T(8,128)S(1)}, f32[512,16]{0,1:T(8,128)}, u32[]{:S(2)}) copy-start(f32[512,16]{0,1:T(8,128)} %param.19) | copy-start | bytes 98308
  7.2 105.7 %all-gather.3.cloned.1.call-start = ((), (), s32[]{:S(2)}) async-start(), calls=%async_computation.4 | async-start | bytes 4456448 | tf_op jit(solution)/shard_map/all_gather | solution.py:106
  14.5 98.4 %copy-start.2 = (bf16[2,512,128]{2,1,0:T(8,128)(2,1)S(1)}, bf16[2,512,128]{2,1,0:T(8,128)(2,1)}, u32[]{:S(2)}) copy-start(bf16[2,512,128]{2,1,0:T(8,128)(2,1)} %param.20) | copy-start | bytes 786436
  54.2 62.1 %copy-start.1 = (bf16[2,128,512]{2,1,0:T(8,128)(2,1)S(1)}, bf16[2,128,512]{2,1,0:T(8,128)(2,1)}, u32[]{:S(2)}) copy-start(bf16[2,128,512]{2,1,0:T(8,128)(2,1)} %param.21) | copy-start | bytes 786436
  54.2 156.5 %reduce-scatter.2.cloned.1.call-start = ((), (), s32[]{:S(2)}) async-start(), calls=%async_computation.5 | async-start | bytes 4456448 | tf_op jit(solution)/shard_map/reduce_scatter | solution.py:113
  119.6 163.3 %all-gather.5.cloned.1.call-start = ((), (), s32[]{:S(2)}) async-start(), calls=%async_computation.6 | async-start | bytes 4456448 | tf_op jit(solution)/shard_map/all_gather | solution.py:107
  119.7 163.2 %copy-start.5 = (bf16[2,128,512]{2,1,0:T(8,128)(2,1)S(1)}, bf16[2,128,512]{2,1,0:T(8,128)(2,1)}, u32[]{:S(2)}) copy-start(bf16[2,128,512]{2,1,0:T(8,128)(2,1)} %param.25) | copy-start | bytes 786436
  119.7 163.2 %copy-start.6 = (bf16[2,128,512]{2,1,0:T(8,128)(2,1)S(1)}, bf16[2,128,512]{2,1,0:T(8,128)(2,1)}, u32[]{:S(2)}) copy-start(bf16[2,128,512]{2,1,0:T(8,128)(2,1)} %param.24) | copy-start | bytes 786436
  212.6 82.1 %all-to-all-start.1 = ((bf16[2,32,4,512]{3,2,0,1:T(4,128)(2,1)}), bf16[2,32,4,512]{3,2,0,1:T(4,128)(2,1)S(1)}, u32[]{:S(2)}, u32[]{:S(2)}) async-start(bf16[2,32,4,512]{3,2,0,1:T(4,128)(2,1)} %copy.31), calls=%async_computation.2 | async-start | bytes 524288 | tf_op jit(solution)/shard_map/all_to_all | solution.py:122
  294.7 1.0 copy-start.3
  294.7 1.5 copy-start.4
Sparse Core Ops, SparseCore 0:
  54.4 58.5 all-gather.2
  119.7 91.0 reduce-scatter.1
  214.8 68.0 all-gather.4
where the time goes:
time: 304 us; the launch traced here: 303 us
  waiting for transfers between devices  169 us (56%)
  blocking collectives  73.5 us (24%)
  matrix products  18.9 us (6%)
  starting transfers between devices  14.8 us (5%)
  between operations  14 us (5%)
  local copies, waits for them, and re-layouts  10 us (3%)
    all_gather x1, waiting for transfers between devices, local(): piece_x = lax.all_gather(recv_x, 'dp', axis=1, tiled=True)  58.6 us
    all_gather x1, waiting for transfers between devices, local(): piece_grad = lax.all_gather(recv_grad, 'dp', axis=1, tiled=True)  55.6 us
    reduce_scatter x1, waiting for transfers between devices, local(): lax.psum_scatter(jnp.einsum('rkf,kfd->rkd', hidden_all, w_down, preferred...  55.1 us
    all_to_all x1, blocking collectives, local(): lax.all_to_all(send_x, 'expert', split_axis=1, concat_axis=1, tiled=True)  38.5 us
    all_to_all x1, blocking collectives, local(): lax.all_to_all(send_grad, 'expert', split_axis=1, concat_axis=1, tiled=True)  34.9 us
    all_to_all x1, starting transfers between devices, local(): lax.all_to_all(outgoing, 'expert', split_axis=1, concat_axis=1, tiled=True)  14.6 us
    dot_general x1, matrix products, outer_in(): jnp.einsum('krd,krf->kdf', rows_x, hidden_grad, preferred_element_type=jn...  7.45 us
  transfers between devices with their start and end apart: 4, of which 3 were waited for; matrix products, arithmetic and copies ran while one was open for 5% of the time, Pallas kernels for 0%

commit v1 on v0

--- a/solution.py
+++ b/solution.py
@@ -10,6 +10,19 @@
 correct_second = 1.0 - 0.95**20
 learn_rate = 0.002
 adam_epsilon = 1e-08
+
+
+def collect(value, axis, dim):
+    ways = lax.axis_size(axis)
+    up = [(d, (d + 1) % ways) for d in range(ways)]
+    down = [(d, (d - 1) % ways) for d in range(ways)]
+    earlier, later = ([value], [value])
+    for _ in range(ways // 2):
+        earlier.append(lax.ppermute(earlier[-1], axis, up))
+    for _ in range((ways - 1) // 2):
+        later.append(lax.ppermute(later[-1], axis, down))
+    line = jnp.concatenate([*earlier[::-1], *later[1:]], axis=dim)
+    return jnp.roll(line, (lax.axis_index(axis) - ways // 2) * value.shape[dim], axis=dim)
 
 
 def gelu_parts(pre):
@@ -103,7 +116,7 @@
     )
     recv_x = recv_x.reshape(local_count, recv_rows, width)
     recv_grad = recv_grad.reshape(local_count, recv_rows, width)
-    piece_x = lax.all_gather(recv_x, "dp", axis=1, tiled=True)
+    piece_x = collect(recv_x, "dp", 1)
     piece_grad = lax.all_gather(recv_grad, "dp", axis=1, tiled=True)
     hidden, hidden_grad = expert_rows(piece_x, piece_grad, w_up, w_down)
     grad_in = outer_in(piece_x, hidden_grad)

time: 304 us -> 341 us (1.12)
  starting transfers between devices: 14.8 us -> 78.3 us
  waiting for transfers between devices: 169 us -> 135 us
  local copies, waits for them, and re-layouts: 10 us -> 17 us
    ppermute x0 -> x15, starting transfers between devices: none -> 63.4 us  [the longest x7 46.9 us: collect(): later.append(lax.ppermute(later[-1], axis, down))]
    all_gather x1 -> x0, waiting for transfers between devices: 58.6 us -> none  [local(): piece_x = lax.all_gather(recv_x, 'dp', axis=1, tiled=True)]
    ppermute x0 -> x15, waiting for transfers between devices: none -> 23 us  [the longest x8 23 us: collect(): earlier.append(lax.ppermute(earlier[-1], axis, up))]
    unnamed x14 -> x53, local copies, waits for them, and re-layouts: 0.04 us -> 7.69 us
  transfers between devices with their start and end apart: 4 -> 18, of which waited for: 3 -> 10; matrix products, arithmetic and copies ran while one was open for 5% -> 5% of each run, Pallas kernels for 0% -> 0%
where the time goes in v1:
time: 341 us; the launch traced here: 340 us
  waiting for transfers between devices  135 us (40%)
  starting transfers between devices  78.3 us (23%)
  blocking collectives  74.8 us (22%)
  local copies, waits for them, and re-layouts  17 us (5%)
  matrix products  16.8 us (5%)
  between operations  14.7 us (4%)
  other arithmetic  3.52 us (1%)
    reduce_scatter x1, waiting for transfers between devices, local(): lax.psum_scatter(jnp.einsum('rkf,kfd->rkd', hidden_all, w_down, preferred...  56.2 us
    all_gather x1, waiting for transfers between devices, local(): piece_grad = lax.all_gather(recv_grad, 'dp', axis=1, tiled=True)  55.5 us
    ppermute x7, starting transfers between devices, collect(): later.append(lax.ppermute(later[-1], axis, down))  46.9 us
    all_to_all x1, blocking collectives, local(): lax.all_to_all(send_x, 'expert', split_axis=1, concat_axis=1, tiled=True)  38.5 us
    all_to_all x1, blocking collectives, local(): lax.all_to_all(send_grad, 'expert', split_axis=1, concat_axis=1, tiled=True)  36.3 us
    ppermute x8, waiting for transfers between devices, collect(): earlier.append(lax.ppermute(earlier[-1], axis, up))  23 us
    ppermute x8, starting transfers between devices, collect(): earlier.append(lax.ppermute(earlier[-1], axis, up))  16.5 us
    all_to_all x1, starting transfers between devices, local(): lax.all_to_all(outgoing, 'expert', split_axis=1, concat_axis=1, tiled=True)  14.8 us
  transfers between devices with their start and end apart: 18, of which 10 were waited for; matrix products, arithmetic and copies ran while one was open for 5% of the time, Pallas kernels for 0%

profile of v1, /device:TPU:1, one launch (start us, length us, event | category | flops | bytes accessed | tf_op | source)
XLA Modules:
  0.0 339.8 jit_solution(8631079735696746325)
XLA Ops:
  7.2 0.8 select_reduce_fusion.2
  8.0 0.8 select_reduce_fusion.1
  8.8 0.1 fusion.35
  8.9 0.2 reduce_window_sum.11
  9.1 0.2 select_reduce_fusion
  9.3 1.0 scatter_custom_fusion
  10.3 0.9 concatenate.12
  11.3 0.9 concatenate.14
  12.2 1.2 gather_fusion.1
  13.3 1.2 gather_fusion.2
  14.5 0.8 broadcast_select_fusion
  15.3 0.1 reshape.141
  15.4 0.1 copy.29
  15.5 38.5 %all_to_all.15 = bf16[2,32,4,512]{3,2,0,1:T(4,128)(2,1)S(1)} all-to-all(bf16[2,32,4,512]{3,2,0,1:T(4,128)(2,1)S(1)} %copy.29), channel_id=1, replica_groups=mesh['dp'=16,'expert'=32] {'expert'}, dimensions={1} | all-to-all | bytes 524288 | tf_op jit(solution)/shard_map/all_to_all | solution.py:114
  54.0 0.1 copy.30
  54.1 0.1 reshape.142
  54.2 3.1 collective-permute-start
  57.3 9.2 %collective-permute-done = bf16[2,128,512]{2,1,0:T(8,128)(2,1)S(1)} collective-permute-done((bf16[2,128,512]{2,1,0:T(8,128)(2,1)S(1)}, bf16[2,128,512]{2,1,0:T(8,128)(2,1)S(1)}, u32[]{:S(2)}, u32[]{:S(2)}) %collective-permute-start) | collective-permute-done | bytes 262176 | tf_op jit(solution)/shard_map/ppermute | solution.py:21
  66.5 1.9 collective-permute-start.1
  68.5 6.7 %collective-permute-start.8 = (bf16[2,128,512]{2,1,0:T(8,128)(2,1)S(1)}, bf16[2,128,512]{2,1,0:T(8,128)(2,1)S(1)}, u32[]{:S(2)}, u32[]{:S(2)}) collective-permute-start(bf16[2,128,512]{2,1,0:T(8,128)(2,1)S(1)} %reshape.142), channel_id=1, source_target_pairs={{0,480},{32,0},{64,32},{96,64},{128,96},{160,128},{192,160},{224,1... | collective-permute-start | bytes 786440 | tf_op jit(solution)/shard_map/ppermute | solution.py:23
  75.2 2.7 collective-permute-done.1
  77.8 1.9 collective-permute-start.2
  79.7 6.7 %collective-permute-start.9 = (bf16[2,128,512]{2,1,0:T(8,128)(2,1)S(1)}, bf16[2,128,512]{2,1,0:T(8,128)(2,1)S(1)}, u32[]{:S(2)}, u32[]{:S(2)}) collective-permute-start(bf16[2,128,512]{2,1,0:T(8,128)(2,1)S(1)} %collective-permute-done.8), channel_id=1, source_target_pairs={{0,480},{32,0},{64,32},{96,64},{128,96},{160,128},{192,160},{224,1... | collective-permute-start | bytes 786440 | tf_op jit(solution)/shard_map/ppermute | solution.py:23
  86.4 1.8 collective-permute-done.2
  88.2 1.9 collective-permute-start.3
  90.2 6.7 %collective-permute-start.10 = (bf16[2,128,512]{2,1,0:T(8,128)(2,1)S(1)}, bf16[2,128,512]{2,1,0:T(8,128)(2,1)S(1)}, u32[]{:S(2)}, u32[]{:S(2)}) collective-permute-start(bf16[2,128,512]{2,1,0:T(8,128)(2,1)S(1)} %collective-permute-done.9), channel_id=1, source_target_pairs={{0,480},{32,0},{64,32},{96,64},{128,96},{160,128},{192,160},{224,1... | collective-permute-start | bytes 786440 | tf_op jit(solution)/shard_map/ppermute | solution.py:23
  96.8 1.8 collective-permute-done.3
  98.7 1.9 collective-permute-start.4
  100.6 6.7 %collective-permute-start.11 = (bf16[2,128,512]{2,1,0:T(8,128)(2,1)S(1)}, bf16[2,128,512]{2,1,0:T(8,128)(2,1)S(1)}, u32[]{:S(2)}, u32[]{:S(2)}) collective-permute-start(bf16[2,128,512]{2,1,0:T(8,128)(2,1)S(1)} %collective-permute-done.10), channel_id=1, source_target_pairs={{0,480},{32,0},{64,32},{96,64},{128,96},{160,128},{192,160},{224,1... | collective-permute-start | bytes 786440 | tf_op jit(solution)/shard_map/ppermute | solution.py:23
  107.3 1.8 collective-permute-done.4
  109.1 1.9 collective-permute-start.5
  111.0 6.7 %collective-permute-start.12 = (bf16[2,128,512]{2,1,0:T(8,128)(2,1)S(1)}, bf16[2,128,512]{2,1,0:T(8,128)(2,1)S(1)}, u32[]{:S(2)}, u32[]{:S(2)}) collective-permute-start(bf16[2,128,512]{2,1,0:T(8,128)(2,1)S(1)} %collective-permute-done.11), channel_id=1, source_target_pairs={{0,480},{32,0},{64,32},{96,64},{128,96},{160,128},{192,160},{224,1... | collective-permute-start | bytes 786440 | tf_op jit(solution)/shard_map/ppermute | solution.py:23
  117.7 1.8 collective-permute-done.5
  119.5 1.9 collective-permute-start.6
  121.4 6.7 %collective-permute-start.13 = (bf16[2,128,512]{2,1,0:T(8,128)(2,1)S(1)}, bf16[2,128,512]{2,1,0:T(8,128)(2,1)S(1)}, u32[]{:S(2)}, u32[]{:S(2)}) collective-permute-start(bf16[2,128,512]{2,1,0:T(8,128)(2,1)S(1)} %collective-permute-done.12), channel_id=1, source_target_pairs={{0,480},{32,0},{64,32},{96,64},{128,96},{160,128},{192,160},{224,1... | collective-permute-start | bytes 786440 | tf_op jit(solution)/shard_map/ppermute | solution.py:23
  128.1 1.9 collective-permute-done.6
  130.0 1.9 collective-permute-start.7
  132.0 6.8 %collective-permute-start.14 = (bf16[2,128,512]{2,1,0:T(8,128)(2,1)S(1)}, bf16[2,128,512]{2,1,0:T(8,128)(2,1)S(1)}, u32[]{:S(2)}, u32[]{:S(2)}) collective-permute-start(bf16[2,128,512]{2,1,0:T(8,128)(2,1)S(1)} %collective-permute-done.13), channel_id=1, source_target_pairs={{0,480},{32,0},{64,32},{96,64},{128,96},{160,128},{192,160},{224,1... | collective-permute-start | bytes 786440 | tf_op jit(solution)/shard_map/ppermute | solution.py:23
  138.8 2.0 collective-permute-done.7
  140.8 1.0 constant_dynamic-update-slice_fusion.31
  141.8 1.0 constant_dynamic-update-slice_fusion.30
  143.1 1.0 constant_dynamic-update-slice_fusion.15
  144.1 1.0 constant_dynamic-update-slice_fusion.14
  145.5 3.2 copy-done.1
  148.7 1.3 fusion.2
  150.0 3.2 convert_bitcast_fusion
  153.2 0.0 all-gather.2.cloned.1.call-start
  153.3 0.1 reshape.145
  153.4 0.1 copy.33
  153.5 36.3 %all_to_all.16 = bf16[2,32,4,512]{3,2,0,1:T(4,128)(2,1)S(1)} all-to-all(bf16[2,32,4,512]{3,2,0,1:T(4,128)(2,1)S(1)} %copy.33), channel_id=1, replica_groups=mesh['dp'=16,'expert'=32] {'expert'}, dimensions={1} | all-to-all | bytes 524288 | tf_op jit(solution)/shard_map/all_to_all | solution.py:115
  189.7 0.1 copy.34
  189.8 0.8 reshape.146
  190.7 56.2 %reduce-scatter.2.cloned.1.call-done = bf16[128,2,512]{2,0,1:T(8,128)(2,1)} async-done(((bf16[2048,2,512]{2,0,1:T(8,128)(2,1)}), bf16[128,2,512]{2,0,1:T(8,128)(2,1)}) %reduce-scatter.2.cloned.1.call-update) | async-done | bytes 262160 | tf_op jit(solution)/shard_map/reduce_scatter | solution.py:126
  246.9 1.0 reshape.143
  247.9 0.8 copy.31
  248.7 14.8 %all-to-all-start.1 = ((bf16[2,32,4,512]{3,2,0,1:T(4,128)(2,1)}), bf16[2,32,4,512]{3,2,0,1:T(4,128)(2,1)S(1)}, u32[]{:S(2)}, u32[]{:S(2)}) async-start(bf16[2,32,4,512]{3,2,0,1:T(4,128)(2,1)} %copy.31), calls=%async_computation.2 | async-start | bytes 524288 | tf_op jit(solution)/shard_map/all_to_all | solution.py:135
  263.5 55.5 %all-gather.2.cloned.1.call-done = bf16[2,2048,512]{2,1,0:T(8,128)(2,1)} async-done(((bf16[2,128,512]{2,1,0:T(8,128)(2,1)}), bf16[2,2048,512]{2,1,0:T(8,128)(2,1)}) %all-gather.2.cloned.1.call-update) | async-done | bytes 4194320 | tf_op jit(solution)/shard_map/all_gather | solution.py:120
  319.0 4.4 %fusion.26 = (bf16[2,128,512]{2,1,0:T(8,128)(2,1)}, bf16[2,128,512]{2,1,0:T(8,128)(2,1)}, bf16[2,128,512]{2,1,0:T(8,128)(2,1)}) fusion(bf16[2,128,512]{2,1,0:T(8,128)(2,1)S(1)} %copy-done.9, bf16[2,128,512]{2,1,0:T(8,128)(2,1)S(1)} %copy-done.10, bf16[2,128,512]{2,1,0:T(8,128)(2,1)S(1)} %copy-done.4, ...), kind=kOutput, calls=%fused_computation.40 | convolution fusion | flops 541982720 | bytes 7864320 | tf_op jit(solution)/shard_map/krf,krd->kfd/dot_general | solution.py:84
  323.4 7.5 %fusion.27 = (bf16[2,512,128]{2,1,0:T(8,128)(2,1)}, bf16[2,512,128]{2,1,0:T(8,128)(2,1)}, bf16[2,512,128]{2,1,0:T(8,128)(2,1)}) fusion(bf16[2,512,128]{2,1,0:T(8,128)(2,1)} %param.23, bf16[2,512,128]{2,1,0:T(8,128)(2,1)} %param.22, bf16[2,512,128]{2,1,0:T(8,128)(2,1)S(1)} %copy-done.6, f32[2,2048,128]{2,1,0:T(8,128)S(1)} %fusion.2, ...), kind=kOutput, calls=%fused_computation.41 | convolution fusion | flops 1081475072 | bytes 12320772 | tf_op jit(solution)/shard_map/krd,krf->kdf/dot_general | solution.py:80
  330.9 0.1 copy.32
  331.0 0.1 reshape.144
  331.0 0.8 gather_fusion
  331.9 0.5 fusion.54
  332.4 0.6 multiply_divide_fusion
  (67 shorter events, 0.8 us)
Async XLA Ops:
  7.2 324.7 %copy-start = (f32[512,16]{0,1:T(8,128)S(1)}, f32[512,16]{0,1:T(8,128)}, u32[]{:S(2)}) copy-start(f32[512,16]{0,1:T(8,128)} %param.19) | copy-start | bytes 98308
  7.2 239.7 %reduce-scatter.2.cloned.1.call-start = ((), (), s32[]{:S(2)}) async-start(), calls=%async_computation.4 | async-start | bytes 4456448 | tf_op jit(solution)/shard_map/reduce_scatter | solution.py:126
  54.2 12.4 %collective-permute-start = (bf16[2,128,512]{2,1,0:T(8,128)(2,1)S(1)}, bf16[2,128,512]{2,1,0:T(8,128)(2,1)S(1)}, u32[]{:S(2)}, u32[]{:S(2)}) collective-permute-start(bf16[2,128,512]{2,1,0:T(8,128)(2,1)S(1)} %reshape.142), channel_id=1, source_target_pairs={{0,32},{32,64},{64,96},{96,128},{128,160},{160,192},{192,224},{224... | collective-permute-start | bytes 786440 | tf_op jit(solution)/shard_map/ppermute | solution.py:21
  66.5 11.3 %collective-permute-start.1 = (bf16[2,128,512]{2,1,0:T(8,128)(2,1)S(1)}, bf16[2,128,512]{2,1,0:T(8,128)(2,1)S(1)}, u32[]{:S(2)}, u32[]{:S(2)}) collective-permute-start(bf16[2,128,512]{2,1,0:T(8,128)(2,1)S(1)} %collective-permute-done), channel_id=1, source_target_pairs={{0,32},{32,64},{64,96},{96,128},{128,160},{160,192},{192,224},{224... | collective-permute-start | bytes 786440 | tf_op jit(solution)/shard_map/ppermute | solution.py:21
  68.5 11.3 %collective-permute-start.8 = (bf16[2,128,512]{2,1,0:T(8,128)(2,1)S(1)}, bf16[2,128,512]{2,1,0:T(8,128)(2,1)S(1)}, u32[]{:S(2)}, u32[]{:S(2)}) collective-permute-start(bf16[2,128,512]{2,1,0:T(8,128)(2,1)S(1)} %reshape.142), channel_id=1, source_target_pairs={{0,480},{32,0},{64,32},{96,64},{128,96},{160,128},{192,160},{224,1... | collective-permute-start | bytes 786440 | tf_op jit(solution)/shard_map/ppermute | solution.py:23
  77.8 10.4 %collective-permute-start.2 = (bf16[2,128,512]{2,1,0:T(8,128)(2,1)S(1)}, bf16[2,128,512]{2,1,0:T(8,128)(2,1)S(1)}, u32[]{:S(2)}, u32[]{:S(2)}) collective-permute-start(bf16[2,128,512]{2,1,0:T(8,128)(2,1)S(1)} %collective-permute-done.1), channel_id=1, source_target_pairs={{0,32},{32,64},{64,96},{96,128},{128,160},{160,192},{192,224},{224... | collective-permute-start | bytes 786440 | tf_op jit(solution)/shard_map/ppermute | solution.py:21
  79.7 10.4 %collective-permute-start.9 = (bf16[2,128,512]{2,1,0:T(8,128)(2,1)S(1)}, bf16[2,128,512]{2,1,0:T(8,128)(2,1)S(1)}, u32[]{:S(2)}, u32[]{:S(2)}) collective-permute-start(bf16[2,128,512]{2,1,0:T(8,128)(2,1)S(1)} %collective-permute-done.8), channel_id=1, source_target_pairs={{0,480},{32,0},{64,32},{96,64},{128,96},{160,128},{192,160},{224,1... | collective-permute-start | bytes 786440 | tf_op jit(solution)/shard_map/ppermute | solution.py:23
  88.2 10.4 %collective-permute-start.3 = (bf16[2,128,512]{2,1,0:T(8,128)(2,1)S(1)}, bf16[2,128,512]{2,1,0:T(8,128)(2,1)S(1)}, u32[]{:S(2)}, u32[]{:S(2)}) collective-permute-start(bf16[2,128,512]{2,1,0:T(8,128)(2,1)S(1)} %collective-permute-done.2), channel_id=1, source_target_pairs={{0,32},{32,64},{64,96},{96,128},{128,160},{160,192},{192,224},{224... | collective-permute-start | bytes 786440 | tf_op jit(solution)/shard_map/ppermute | solution.py:21
  90.2 10.4 %collective-permute-start.10 = (bf16[2,128,512]{2,1,0:T(8,128)(2,1)S(1)}, bf16[2,128,512]{2,1,0:T(8,128)(2,1)S(1)}, u32[]{:S(2)}, u32[]{:S(2)}) collective-permute-start(bf16[2,128,512]{2,1,0:T(8,128)(2,1)S(1)} %collective-permute-done.9), channel_id=1, source_target_pairs={{0,480},{32,0},{64,32},{96,64},{128,96},{160,128},{192,160},{224,1... | collective-permute-start | bytes 786440 | tf_op jit(solution)/shard_map/ppermute | solution.py:23
  98.7 10.4 %collective-permute-start.4 = (bf16[2,128,512]{2,1,0:T(8,128)(2,1)S(1)}, bf16[2,128,512]{2,1,0:T(8,128)(2,1)S(1)}, u32[]{:S(2)}, u32[]{:S(2)}) collective-permute-start(bf16[2,128,512]{2,1,0:T(8,128)(2,1)S(1)} %collective-permute-done.3), channel_id=1, source_target_pairs={{0,32},{32,64},{64,96},{96,128},{128,160},{160,192},{192,224},{224... | collective-permute-start | bytes 786440 | tf_op jit(solution)/shard_map/ppermute | solution.py:21
  100.6 10.4 %collective-permute-start.11 = (bf16[2,128,512]{2,1,0:T(8,128)(2,1)S(1)}, bf16[2,128,512]{2,1,0:T(8,128)(2,1)S(1)}, u32[]{:S(2)}, u32[]{:S(2)}) collective-permute-start(bf16[2,128,512]{2,1,0:T(8,128)(2,1)S(1)} %collective-permute-done.10), channel_id=1, source_target_pairs={{0,480},{32,0},{64,32},{96,64},{128,96},{160,128},{192,160},{224,1... | collective-permute-start | bytes 786440 | tf_op jit(solution)/shard_map/ppermute | solution.py:23
  109.1 10.4 %collective-permute-start.5 = (bf16[2,128,512]{2,1,0:T(8,128)(2,1)S(1)}, bf16[2,128,512]{2,1,0:T(8,128)(2,1)S(1)}, u32[]{:S(2)}, u32[]{:S(2)}) collective-permute-start(bf16[2,128,512]{2,1,0:T(8,128)(2,1)S(1)} %collective-permute-done.4), channel_id=1, source_target_pairs={{0,32},{32,64},{64,96},{96,128},{128,160},{160,192},{192,224},{224... | collective-permute-start | bytes 786440 | tf_op jit(solution)/shard_map/ppermute | solution.py:21
  111.0 10.4 %collective-permute-start.12 = (bf16[2,128,512]{2,1,0:T(8,128)(2,1)S(1)}, bf16[2,128,512]{2,1,0:T(8,128)(2,1)S(1)}, u32[]{:S(2)}, u32[]{:S(2)}) collective-permute-start(bf16[2,128,512]{2,1,0:T(8,128)(2,1)S(1)} %collective-permute-done.11), channel_id=1, source_target_pairs={{0,480},{32,0},{64,32},{96,64},{128,96},{160,128},{192,160},{224,1... | collective-permute-start | bytes 786440 | tf_op jit(solution)/shard_map/ppermute | solution.py:23
  119.5 10.5 %collective-permute-start.6 = (bf16[2,128,512]{2,1,0:T(8,128)(2,1)S(1)}, bf16[2,128,512]{2,1,0:T(8,128)(2,1)}, u32[]{:S(2)}, u32[]{:S(2)}) collective-permute-start(bf16[2,128,512]{2,1,0:T(8,128)(2,1)S(1)} %collective-permute-done.5), channel_id=1, source_target_pairs={{0,32},{32,64},{64,96},{96,128},{128,160},{160,192},{192,224},{224... | collective-permute-start | bytes 786440 | tf_op jit(solution)/shard_map/ppermute | solution.py:21
  121.4 10.6 %collective-permute-start.13 = (bf16[2,128,512]{2,1,0:T(8,128)(2,1)S(1)}, bf16[2,128,512]{2,1,0:T(8,128)(2,1)S(1)}, u32[]{:S(2)}, u32[]{:S(2)}) collective-permute-start(bf16[2,128,512]{2,1,0:T(8,128)(2,1)S(1)} %collective-permute-done.12), channel_id=1, source_target_pairs={{0,480},{32,0},{64,32},{96,64},{128,96},{160,128},{192,160},{224,1... | collective-permute-start | bytes 786440 | tf_op jit(solution)/shard_map/ppermute | solution.py:23
  130.0 10.7 %collective-permute-start.7 = (bf16[2,128,512]{2,1,0:T(8,128)(2,1)}, bf16[2,128,512]{2,1,0:T(8,128)(2,1)}, u32[]{:S(2)}, u32[]{:S(2)}) collective-permute-start(bf16[2,128,512]{2,1,0:T(8,128)(2,1)} %collective-permute-done.6), channel_id=1, source_target_pairs={{0,32},{32,64},{64,96},{96,128},{128,160},{160,192},{192,224},{224... | collective-permute-start | bytes 786440 | tf_op jit(solution)/shard_map/ppermute | solution.py:21
  132.0 16.7 %copy-start.5 = (bf16[2,512,128]{2,1,0:T(8,128)(2,1)S(1)}, bf16[2,512,128]{2,1,0:T(8,128)(2,1)}, u32[]{:S(2)}) copy-start(bf16[2,512,128]{2,1,0:T(8,128)(2,1)} %param.20) | copy-start | bytes 786436
  132.0 11.1 %collective-permute-start.14 = (bf16[2,128,512]{2,1,0:T(8,128)(2,1)S(1)}, bf16[2,128,512]{2,1,0:T(8,128)(2,1)S(1)}, u32[]{:S(2)}, u32[]{:S(2)}) collective-permute-start(bf16[2,128,512]{2,1,0:T(8,128)(2,1)S(1)} %collective-permute-done.13), channel_id=1, source_target_pairs={{0,480},{32,0},{64,32},{96,64},{128,96},{160,128},{192,160},{224,1... | collective-permute-start | bytes 786440 | tf_op jit(solution)/shard_map/ppermute | solution.py:23
  143.0 7.0 %copy-start.3 = (bf16[2,128,512]{2,1,0:T(8,128)(2,1)S(1)}, bf16[2,128,512]{2,1,0:T(8,128)(2,1)}, u32[]{:S(2)}) copy-start(bf16[2,128,512]{2,1,0:T(8,128)(2,1)} %param.21) | copy-start | bytes 786436
  145.5 3.2 copy-start.1
  148.7 4.6 %copy-start.2 = (bf16[256,512]{1,0:T(8,128)(2,1)S(1)}, bf16[256,512]{1,0:T(8,128)(2,1)}, u32[]{:S(2)}) copy-start(bf16[256,512]{1,0:T(8,128)(2,1)} %get-tuple-element.14) | copy-start | bytes 786436
  150.0 169.0 %copy-start.4 = (bf16[2,128,512]{2,1,0:T(8,128)(2,1)S(1)}, bf16[2,128,512]{2,1,0:T(8,128)(2,1)}, u32[]{:S(2)}) copy-start(bf16[2,128,512]{2,1,0:T(8,128)(2,1)} %param.21) | copy-start | bytes 786436
  150.0 169.0 %copy-start.9 = (bf16[2,128,512]{2,1,0:T(8,128)(2,1)S(1)}, bf16[2,128,512]{2,1,0:T(8,128)(2,1)}, u32[]{:S(2)}) copy-start(bf16[2,128,512]{2,1,0:T(8,128)(2,1)} %param.25) | copy-start | bytes 786436
  150.0 169.0 %copy-start.10 = (bf16[2,128,512]{2,1,0:T(8,128)(2,1)S(1)}, bf16[2,128,512]{2,1,0:T(8,128)(2,1)}, u32[]{:S(2)}) copy-start(bf16[2,128,512]{2,1,0:T(8,128)(2,1)} %param.24) | copy-start | bytes 786436
  153.2 165.7 %all-gather.2.cloned.1.call-start = ((), (), s32[]{:S(2)}) async-start(), calls=%async_computation.5 | async-start | bytes 4456448 | tf_op jit(solution)/shard_map/all_gather | solution.py:120
  248.7 74.7 %copy-start.6 = (bf16[2,512,128]{2,1,0:T(8,128)(2,1)S(1)}, bf16[2,512,128]{2,1,0:T(8,128)(2,1)}, u32[]{:S(2)}) copy-start(bf16[2,512,128]{2,1,0:T(8,128)(2,1)} %param.20) | copy-start | bytes 786436
  248.7 82.2 %all-to-all-start.1 = ((bf16[2,32,4,512]{3,2,0,1:T(4,128)(2,1)}), bf16[2,32,4,512]{3,2,0,1:T(4,128)(2,1)S(1)}, u32[]{:S(2)}, u32[]{:S(2)}) async-start(bf16[2,32,4,512]{3,2,0,1:T(4,128)(2,1)} %copy.31), calls=%async_computation.2 | async-start | bytes 524288 | tf_op jit(solution)/shard_map/all_to_all | solution.py:135
  323.3 8.5 %copy-start.7 = (bf16[128,512]{1,0:T(8,128)(2,1)S(1)}, bf16[128,512]{1,0:T(8,128)(2,1)}, u32[]{:S(2)}) copy-start(bf16[128,512]{1,0:T(8,128)(2,1)} %param.14) | copy-start | bytes 393220
  323.4 9.0 %copy-start.8 = (f32[128]{0:T(128)S(1)}, f32[128]{0:T(128)}, u32[]{:S(2)}) copy-start(f32[128]{0:T(128)} %param.18) | copy-start | bytes 1540
Sparse Core Ops, SparseCore 0:
  153.4 93.4 reduce-scatter.1
  250.9 68.0 all-gather.1
